TPU v7x, 32 devices: a whole 2x2x4 slice. The times are simulated.
32 devices in a mesh: grp: 4 (over y, core), seq: 8 (over z, x).
Axes of the slice: x: 2, y: 2, z: 4, core: 2. Of those that a mesh axis runs over, the one named last changes fastest.
Arguments:
- queries: bfloat16 [16384, 1024], P(('grp', 'seq')), may hold values from -200 to 200
- keys: bfloat16 [16384, 1024], P(('grp', 'seq')), may hold values from -5 to 5
- values: bfloat16 [16384, 1024], P(('grp', 'seq')), may hold values from -6 to 6
- out_grad: bfloat16 [16384, 1024], P(('grp', 'seq')), may hold values from -6 to 6
Outputs:
- attended: bfloat16 [16384, 1024], P(('grp', 'seq'))
- grad_queries: bfloat16 [16384, 1024], P(('grp', 'seq'))
- grad_keys: bfloat16 [16384, 1024], P(('grp', 'seq'))
- grad_values: bfloat16 [16384, 1024], P(('grp', 'seq'))
All inputs are finite; a program needn't handle non-finite values.
Results may differ from a plain program's by a relative error of at most 0.02.
Values may be sent and summed in bfloat16 or wider, within the bound.
A program may use at most 128 MiB of HBM per device.

v0:
```python
import math

import jax
import jax.numpy as jnp
from jax import lax
from jax.sharding import PartitionSpec as P

H = 16
HD = 64
BLOCK = 512
P1 = 4
P2 = 32
RATIO = 8


EPS = 1e-06
NEG = -1e30


def extended(cells, sides, width):
    for axis, dim in sides:
        count = lax.axis_size(axis)
        ends = count - 1
        head = lax.slice_in_dim(cells, 0, width, axis=dim)
        tail = lax.slice_in_dim(cells, cells.shape[dim] - width, cells.shape[dim], axis=dim)
        cells = jnp.concatenate(
            [
                lax.ppermute(tail, axis, [(i, (i + 1) % count) for i in range(ends)]),
                cells,
                lax.ppermute(head, axis, [((i + 1) % count, i) for i in range(ends)]),
            ],
            axis=dim,
        )
    return cells


def shifted(block, axis, distance):
    devices = range(lax.axis_size(axis))
    route = [(i - distance, i) for i in devices if i - distance in devices]
    return lax.ppermute(block, axis, route)


def keep_bf16(value):
    rounded = lax.optimization_barrier(value.astype(jnp.bfloat16)).astype(jnp.float32)
    return value + lax.stop_gradient(rounded - value)


def pool_rows(stacked, factor):
    count_rows = stacked.shape[1] // factor
    return jnp.mean(
        stacked.reshape(2, count_rows, factor, stacked.shape[2]), axis=2, dtype=jnp.float32
    )


def normalize(pooled):
    shaped = pooled.reshape(pooled.shape[:-1] + (H, HD))
    scaled = shaped * lax.rsqrt(jnp.mean(shaped * shaped, axis=-1, keepdims=True) + EPS)
    return keep_bf16(scaled.reshape(pooled.shape))


def summary_back(pooled, upstream, factor):
    unused, pullback = jax.vjp(normalize, pooled)
    return jnp.repeat(pullback(upstream)[0] / factor, factor, axis=1)


def attend_block(query_rows, grad_rows, key_rows, value_rows, key_live):
    score_scale = 1.0 / math.sqrt(HD)
    pair_width = 2 * HD

    def one_pair(pair_index, totals):
        out_total, query_total, key_total, value_total = totals
        offset = pair_index * pair_width

        def take_pair(matrix):
            return lax.dynamic_slice_in_dim(matrix, offset, pair_width, 1).reshape(
                matrix.shape[0], 2, HD
            )

        query_part = take_pair(query_rows)
        grad_part = take_pair(grad_rows)
        key_part = take_pair(key_rows)
        value_part = take_pair(value_rows)
        scores = (
            jnp.einsum("qhd,khd->hqk", query_part, key_part, preferred_element_type=jnp.float32)
            * score_scale
        )
        scores = jnp.where(key_live[None, None, :], scores, NEG)
        largest = jnp.max(scores, axis=-1, keepdims=True)
        unnormed = jnp.exp(scores - largest)
        attn_probs = unnormed / jnp.sum(unnormed, axis=-1, keepdims=True)
        probs_low = attn_probs.astype(jnp.bfloat16)
        out_part = jnp.einsum(
            "hqk,khd->qhd", probs_low, value_part, preferred_element_type=jnp.float32
        )
        prob_grad = jnp.einsum(
            "qhd,khd->hqk", grad_part, value_part, preferred_element_type=jnp.float32
        )
        row_delta = jnp.sum(attn_probs * prob_grad, axis=-1, keepdims=True)
        score_grad = (attn_probs * (prob_grad - row_delta) * score_scale).astype(jnp.bfloat16)
        query_grad = jnp.einsum(
            "hqk,khd->qhd", score_grad, key_part, preferred_element_type=jnp.float32
        )
        key_grad = jnp.einsum(
            "hqk,qhd->khd", score_grad, query_part, preferred_element_type=jnp.float32
        )
        value_grad = jnp.einsum(
            "hqk,qhd->khd", probs_low, grad_part, preferred_element_type=jnp.float32
        )
        rows_q = query_rows.shape[0]
        rows_k = key_rows.shape[0]
        out_total = lax.dynamic_update_slice_in_dim(
            out_total, out_part.reshape(rows_q, pair_width), offset, 1
        )
        query_total = lax.dynamic_update_slice_in_dim(
            query_total, query_grad.reshape(rows_q, pair_width), offset, 1
        )
        key_total = lax.dynamic_update_slice_in_dim(
            key_total, key_grad.reshape(rows_k, pair_width), offset, 1
        )
        value_total = lax.dynamic_update_slice_in_dim(
            value_total, value_grad.reshape(rows_k, pair_width), offset, 1
        )
        return (out_total, query_total, key_total, value_total)

    query_zero = jnp.zeros(query_rows.shape, jnp.float32)
    key_zero = jnp.zeros(key_rows.shape, jnp.float32)
    return lax.fori_loop(0, H // 2, one_pair, (query_zero, query_zero, key_zero, key_zero))


def per_device(queries, keys, values, out_grad):
    frames = queries.shape[0]
    width_all = queries.shape[1]
    blocks = frames // BLOCK
    near_len = BLOCK // P1
    seq_count = lax.axis_size("seq")
    grp_count = lax.axis_size("grp")
    device = lax.axis_index("grp") * seq_count + lax.axis_index("seq")
    total_blocks = blocks * seq_count * grp_count
    stacked_kv = jnp.stack([keys, values])
    near_pooled = pool_rows(stacked_kv, P1)
    near_local = normalize(near_pooled).astype(jnp.bfloat16)
    near_ext = extended(near_local, ((("grp", "seq"), 1),), near_len)
    group_pooled = pool_rows(stacked_kv, P2)
    group_local = normalize(group_pooled).astype(jnp.bfloat16)
    group_all = lax.all_gather(group_local, "seq", axis=1, tiled=True)
    top_pooled = pool_rows(group_local, RATIO)
    top_local = normalize(top_pooled).astype(jnp.bfloat16)
    top_all = lax.all_gather(top_local, ("grp", "seq"), axis=1, tiled=True)
    group_len = group_all.shape[1]
    top_len = top_all.shape[1]
    key_count = BLOCK + 2 * near_len + group_len + top_len
    position = jnp.arange(key_count, dtype=jnp.int32)
    in_before = jnp.logical_and(position >= BLOCK, position < BLOCK + near_len)
    in_after = jnp.logical_and(position >= BLOCK + near_len, position < BLOCK + 2 * near_len)
    lower = BLOCK + 2 * near_len

    def step(totals, block_index):
        group_grad, top_grad = totals
        before_rows = lax.dynamic_slice_in_dim(near_ext, block_index * near_len, near_len, 1)
        after_rows = lax.dynamic_slice_in_dim(near_ext, (block_index + 2) * near_len, near_len, 1)
        key_sets = jnp.concatenate(
            [stacked_kv, before_rows, after_rows, group_all, top_all], axis=1
        )
        number = device * blocks + block_index
        key_live = jnp.logical_not(
            jnp.logical_or(
                jnp.logical_and(in_before, number == 0),
                jnp.logical_and(in_after, number == total_blocks - 1),
            )
        )
        output, query_grad, key_grad, value_grad = attend_block(
            queries, out_grad, key_sets[0], key_sets[1], key_live
        )
        pair_grad = jnp.stack([key_grad, value_grad])
        group_grad = group_grad + pair_grad[:, lower : lower + group_len]
        top_grad = top_grad + pair_grad[:, lower + group_len :]
        outs = (
            output.astype(jnp.bfloat16),
            query_grad.astype(jnp.bfloat16),
            pair_grad[:, :BLOCK],
            pair_grad[:, BLOCK : BLOCK + near_len],
            pair_grad[:, BLOCK + near_len : lower],
        )
        return ((group_grad, top_grad), outs)

    start_totals = (
        jnp.zeros((2, group_len, width_all), jnp.float32),
        jnp.zeros((2, top_len, width_all), jnp.float32),
    )
    (group_grad, top_grad), stacked_outs = lax.scan(
        step, start_totals, jnp.arange(blocks, dtype=jnp.int32)
    )
    attended_blocks, query_blocks, diag_grads, before_grads, after_grads = stacked_outs
    zero_pad = jnp.zeros((2, 2, near_len, width_all), jnp.float32)
    ext_grads = jnp.concatenate([before_grads, zero_pad]) + jnp.concatenate([zero_pad, after_grads])
    lower_rim = ext_grads[0]
    upper_rim = ext_grads[blocks + 1]
    from_next = shifted(lower_rim.astype(jnp.bfloat16), ("grp", "seq"), -1).astype(lower_rim.dtype)
    from_prev = shifted(upper_rim.astype(jnp.bfloat16), ("grp", "seq"), 1).astype(upper_rim.dtype)
    inner = ext_grads[1 : blocks + 1]
    inner = inner.at[0].add(from_prev)
    inner = inner.at[blocks - 1].add(from_next)
    near_grad = jnp.moveaxis(inner, 1, 0).reshape(2, frames // P1, width_all)
    top_own = lax.psum_scatter(top_grad, ("grp", "seq"), scatter_dimension=1, tiled=True)
    extra = summary_back(top_pooled, top_own, RATIO)
    group_own = (
        lax.psum_scatter(
            group_grad.astype(jnp.bfloat16), "seq", scatter_dimension=1, tiled=True
        ).astype(jnp.float32)
        + extra
    )
    diag_total = jnp.moveaxis(diag_grads, 1, 0).reshape(2, frames, width_all)
    kv_grad = (
        diag_total
        + summary_back(near_pooled, near_grad, P1)
        + summary_back(group_pooled, group_own, P2)
    )
    return (
        attended_blocks.reshape(frames, width_all),
        query_blocks.reshape(frames, width_all),
        kv_grad[0].astype(jnp.bfloat16),
        kv_grad[1].astype(jnp.bfloat16),
    )


def solution(mesh):
    in_specs = (
        P(("grp", "seq"), None),
        P(("grp", "seq"), None),
        P(("grp", "seq"), None),
        P(("grp", "seq"), None),
    )
    out_specs = (
        P(("grp", "seq"), None),
        P(("grp", "seq"), None),
        P(("grp", "seq"), None),
        P(("grp", "seq"), None),
    )
    return jax.shard_map(
        per_device, mesh=mesh, in_specs=in_specs, out_specs=out_specs, check_vma=False
    )
```

profile of v0, /device:TPU:0, one launch (start us, length us, event | category | flops | bytes accessed | tf_op | source)
XLA Modules:
  0.0 715.6 jit_solution(5743291594955407500)
XLA Ops:
  10.1 2.8 convert_reduce_fusion.1
  19.0 6.3 collective-permute-start
  33.6 83.2 %all_gather.7 = bf16[2,64,1024]{2,0,1:T(2,128)(2,1)} all-gather(bf16[2,2,1024]{2,0,1:T(2,128)(2,1)S(1)} %copy.48), channel_id=1, replica_groups=mesh['grp'=4,'seq'=8] {'grp','seq'}, dimensions={1}, use_global_device_ids=true | all-gather | bytes 270336 | tf_op jit(solution)/shard_map/all_gather | solution.py:148
  118.1 2.4 copy.44
  123.8 33.8 %all_gather.6 = bf16[2,128,1024]{2,0,1:T(2,128)(2,1)} all-gather(bf16[2,16,1024]{2,0,1:T(2,128)(2,1)} %copy.47), channel_id=1, replica_groups=mesh['grp'=4,'seq'=8] {'seq'}, dimensions={1}, use_global_device_ids=true | all-gather | bytes 589824 | tf_op jit(solution)/shard_map/all_gather | solution.py:145
  160.3 2.7 maximum_dynamic-update-slice_fusion
  172.9 4.6 slice_bitcast_fusion
  179.7 2.4 broadcast.203.clone2
  182.1 2.4 broadcast.203.clone
  184.5 284.0 %while.38 = (s32[]{:T(128)}, bf16[512,1024]{1,0:T(8,128)(2,1)}, bf16[512,1024]{1,0:T(8,128)(2,1)}, f32[960,1024]{1,0:T(8,128)}, f32[960,1024]{1,0:T(8,128)}, /*i...) while((s32[]{:T(128)}, bf16[512,1024]{1,0:T(8,128)(2,1)}, ...), condition=%wide.region_10.0_spmd.clone, body=%wide.region_6.10_spmd.clone.sunk | while | flops 776616128 | bytes 41244756 | solution.py:127
  188.5 2.7 fusion.111
  191.2 3.5 fusion.113
  194.7 3.2 fusion.115
  197.9 7.0 fusion.114
  204.9 7.8 %fusion.117 = f32[2,64,960]{2,1,0:T(8,128)} fusion(bf16[512,2,64]{0,2,1:T(8,128)(2,1)S(1)} %bitcast.143, f32[2,512,960]{1,2,0:T(8,128)} %fusion.111, f32[2,512,960]{1,2,0:T(8,128)} %get-tuple-element.456, f32[2,512]{1,0:T(2,128)S(1)} %get-tuple-element.457), kind=kOutput, calls=%fused_computation.9.clone.1 | convolution fusion | flops 132712384 | bytes 8491008 | tf_op jit(solution)/shard_map/while/body/eval_jaxpr/while/body/eval_jaxpr/hqk,qhd->khd/dot_general | solution.py:103
  212.7 2.8 fusion.116
  224.0 2.7 fusion.111
  226.7 3.5 fusion.113
  230.2 3.2 fusion.115
  233.5 7.0 fusion.114
  240.5 7.8 %fusion.117 = f32[2,64,960]{2,1,0:T(8,128)} fusion(bf16[512,2,64]{0,2,1:T(8,128)(2,1)S(1)} %bitcast.143, f32[2,512,960]{1,2,0:T(8,128)} %fusion.111, f32[2,512,960]{1,2,0:T(8,128)} %get-tuple-element.456, f32[2,512]{1,0:T(2,128)S(1)} %get-tuple-element.457), kind=kOutput, calls=%fused_computation.9.clone.1 | convolution fusion | flops 132712384 | bytes 8491008 | tf_op jit(solution)/shard_map/while/body/eval_jaxpr/while/body/eval_jaxpr/hqk,qhd->khd/dot_general | solution.py:103
  248.2 2.8 fusion.116
  259.6 2.7 fusion.111
  262.3 3.5 fusion.113
  265.8 3.2 fusion.115
  269.0 7.0 fusion.114
  276.0 7.8 %fusion.117 = f32[2,64,960]{2,1,0:T(8,128)} fusion(bf16[512,2,64]{0,2,1:T(8,128)(2,1)S(1)} %bitcast.143, f32[2,512,960]{1,2,0:T(8,128)} %fusion.111, f32[2,512,960]{1,2,0:T(8,128)} %get-tuple-element.456, f32[2,512]{1,0:T(2,128)S(1)} %get-tuple-element.457), kind=kOutput, calls=%fused_computation.9.clone.1 | convolution fusion | flops 132712384 | bytes 8491008 | tf_op jit(solution)/shard_map/while/body/eval_jaxpr/while/body/eval_jaxpr/hqk,qhd->khd/dot_general | solution.py:103
  283.8 2.8 fusion.116
  295.0 2.7 fusion.111
  297.7 3.5 fusion.113
  301.2 3.2 fusion.115
  304.5 7.0 fusion.114
  311.5 7.8 %fusion.117 = f32[2,64,960]{2,1,0:T(8,128)} fusion(bf16[512,2,64]{0,2,1:T(8,128)(2,1)S(1)} %bitcast.143, f32[2,512,960]{1,2,0:T(8,128)} %fusion.111, f32[2,512,960]{1,2,0:T(8,128)} %get-tuple-element.456, f32[2,512]{1,0:T(2,128)S(1)} %get-tuple-element.457), kind=kOutput, calls=%fused_computation.9.clone.1 | convolution fusion | flops 132712384 | bytes 8491008 | tf_op jit(solution)/shard_map/while/body/eval_jaxpr/while/body/eval_jaxpr/hqk,qhd->khd/dot_general | solution.py:103
  319.2 2.8 fusion.116
  330.5 2.7 fusion.111
  333.2 3.5 fusion.113
  336.7 3.2 fusion.115
  340.0 7.0 fusion.114
  347.0 7.8 %fusion.117 = f32[2,64,960]{2,1,0:T(8,128)} fusion(bf16[512,2,64]{0,2,1:T(8,128)(2,1)S(1)} %bitcast.143, f32[2,512,960]{1,2,0:T(8,128)} %fusion.111, f32[2,512,960]{1,2,0:T(8,128)} %get-tuple-element.456, f32[2,512]{1,0:T(2,128)S(1)} %get-tuple-element.457), kind=kOutput, calls=%fused_computation.9.clone.1 | convolution fusion | flops 132712384 | bytes 8491008 | tf_op jit(solution)/shard_map/while/body/eval_jaxpr/while/body/eval_jaxpr/hqk,qhd->khd/dot_general | solution.py:103
  354.7 2.8 fusion.116
  366.0 2.7 fusion.111
  368.7 3.5 fusion.113
  372.2 3.2 fusion.115
  375.5 7.0 fusion.114
  382.5 7.8 %fusion.117 = f32[2,64,960]{2,1,0:T(8,128)} fusion(bf16[512,2,64]{0,2,1:T(8,128)(2,1)S(1)} %bitcast.143, f32[2,512,960]{1,2,0:T(8,128)} %fusion.111, f32[2,512,960]{1,2,0:T(8,128)} %get-tuple-element.456, f32[2,512]{1,0:T(2,128)S(1)} %get-tuple-element.457), kind=kOutput, calls=%fused_computation.9.clone.1 | convolution fusion | flops 132712384 | bytes 8491008 | tf_op jit(solution)/shard_map/while/body/eval_jaxpr/while/body/eval_jaxpr/hqk,qhd->khd/dot_general | solution.py:103
  390.2 2.8 fusion.116
  401.5 2.7 fusion.111
  404.2 3.5 fusion.113
  407.7 3.2 fusion.115
  410.9 7.0 fusion.114
  418.0 7.8 %fusion.117 = f32[2,64,960]{2,1,0:T(8,128)} fusion(bf16[512,2,64]{0,2,1:T(8,128)(2,1)S(1)} %bitcast.143, f32[2,512,960]{1,2,0:T(8,128)} %fusion.111, f32[2,512,960]{1,2,0:T(8,128)} %get-tuple-element.456, f32[2,512]{1,0:T(2,128)S(1)} %get-tuple-element.457), kind=kOutput, calls=%fused_computation.9.clone.1 | convolution fusion | flops 132712384 | bytes 8491008 | tf_op jit(solution)/shard_map/while/body/eval_jaxpr/while/body/eval_jaxpr/hqk,qhd->khd/dot_general | solution.py:103
  425.7 2.8 fusion.116
  437.0 2.7 fusion.111
  439.7 3.5 fusion.113
  443.2 3.2 fusion.115
  446.5 7.0 fusion.114
  453.5 7.8 %fusion.117 = f32[2,64,960]{2,1,0:T(8,128)} fusion(bf16[512,2,64]{0,2,1:T(8,128)(2,1)S(1)} %bitcast.143, f32[2,512,960]{1,2,0:T(8,128)} %fusion.111, f32[2,512,960]{1,2,0:T(8,128)} %get-tuple-element.456, f32[2,512]{1,0:T(2,128)S(1)} %get-tuple-element.457), kind=kOutput, calls=%fused_computation.9.clone.1 | convolution fusion | flops 132712384 | bytes 8491008 | tf_op jit(solution)/shard_map/while/body/eval_jaxpr/while/body/eval_jaxpr/hqk,qhd->khd/dot_general | solution.py:103
  461.2 2.8 fusion.116
  475.2 2.4 copy.64
  483.8 123.6 %all-reduce.9.cloned.1.call-done = f32[2,64,1024]{2,0,1:T(2,128)} async-done(((f32[2,64,1024]{2,0,1:T(2,128)}), f32[2,64,1024]{2,0,1:T(2,128)}) %all-reduce.9.cloned.1.call-update) | async-done | bytes 524304
  608.6 74.1 %all-reduce.7.cloned.1.call-done = bf16[2,128,1024]{2,0,1:T(2,128)(2,1)} async-done(((bf16[2,128,1024]{2,0,1:T(2,128)(2,1)}), bf16[2,128,1024]{2,0,1:T(2,128)(2,1)}) %all-reduce.7.cloned.1.call-update) | async-done | bytes 524304
  691.2 2.4 fusion.46
  693.6 2.6 copy.60
  699.0 2.6 copy.61
  (218 shorter events, 135.7 us)
Async XLA Ops:
  7.2 600.3 %all-reduce.9.cloned.1.call-start = ((), (), s32[]{:S(2)}) async-start(), calls=%async_computation.1 | async-start | bytes 1048576
  13.4 1.3 copy-start.6
  14.7 10.5 %copy-start.4 = (bf16[512,1024]{1,0:T(8,128)(2,1)S(1)}, bf16[512,1024]{1,0:T(8,128)(2,1)}, u32[]{:S(2)}) copy-start(bf16[512,1024]{1,0:T(8,128)(2,1)} %param.11) | copy-start | bytes 3145732
  16.4 8.9 %copy-start.5 = (bf16[512,1024]{1,0:T(8,128)(2,1)S(1)}, bf16[512,1024]{1,0:T(8,128)(2,1)}, u32[]{:S(2)}) copy-start(bf16[512,1024]{1,0:T(8,128)(2,1)} %param.12) | copy-start | bytes 3145732
  17.7 149.5 %collective-permute-start.1 = (bf16[2,128,1024]{2,1,0:T(8,128)(2,1)}, bf16[2,128,1024]{2,1,0:T(8,128)(2,1)}, u32[]{:S(2)}, u32[]{:S(2)}) collective-permute-start(bf16[2,128,1024]{2,1,0:T(8,128)(2,1)} %fusion.42), channel_id=1, source_target_pairs={{1,0},{2,1},{3,2},{4,3},{5,4},{6,5},{7,6},{8,7},{9,8},{10,9},{11,1... | collective-permute-start | bytes 1572872 | tf_op jit(solution)/shard_map/ppermute | solution.py:30
  19.0 144.1 %collective-permute-start = (bf16[2,128,1024]{2,1,0:T(8,128)(2,1)}, bf16[2,128,1024]{2,1,0:T(8,128)(2,1)}, u32[]{:S(2)}, u32[]{:S(2)}) collective-permute-start(bf16[2,128,1024]{2,1,0:T(8,128)(2,1)} %fusion.42), channel_id=1, source_target_pairs={{0,1},{1,2},{2,3},{3,4},{4,5},{5,6},{6,7},{7,8},{8,9},{9,10},{10,1... | collective-permute-start | bytes 1572872 | tf_op jit(solution)/shard_map/ppermute | solution.py:28
  25.8 94.6 %copy-start.15 = (u32[32]{0:T(128)S(1)}, u32[32]{0:T(128)}, u32[]{:S(2)}) copy-start(u32[32]{0:T(128)} %constant.193) | copy-start | bytes 388
  29.7 130.0 %copy-start.9 = (f32[2,16,1024]{2,1,0:T(8,128)}, f32[2,16,1024]{2,1,0:T(8,128)S(1)}, u32[]{:S(2)}) copy-start(f32[2,16,1024]{2,1,0:T(8,128)S(1)} %mul.200) | copy-start | bytes 393220
  30.4 90.7 %copy-start.14 = (bf16[2,16,1024]{2,1,0:T(8,128)(2,1)S(1)}, bf16[2,16,1024]{2,1,0:T(8,128)(2,1)}, u32[]{:S(2)}) copy-start(bf16[2,16,1024]{2,1,0:T(8,128)(2,1)} %get-tuple-element.368) | copy-start | bytes 196612
  118.1 42.2 %copy-start.8 = (bf16[512,1024]{0,1:T(8,128)(2,1)S(1)}, bf16[512,1024]{0,1:T(8,128)(2,1)}, u32[]{:S(2)}) copy-start(bf16[512,1024]{0,1:T(8,128)(2,1)} %copy.43) | copy-start | bytes 3145732
  163.1 8.1 %copy-start.12 = (bf16[2,128,1024]{1,2,0:T(8,128)(2,1)S(1)}, bf16[2,128,1024]{1,2,0:T(8,128)(2,1)}, u32[]{:S(2)}) copy-start(bf16[2,128,1024]{1,2,0:T(8,128)(2,1)} %copy.51) | copy-start | bytes 1572868
  163.1 8.9 %copy-start.11 = (bf16[2,64,1024]{1,2,0:T(8,128)(2,1)S(1)}, bf16[2,64,1024]{1,2,0:T(8,128)(2,1)}, u32[]{:S(2)}) copy-start(bf16[2,64,1024]{1,2,0:T(8,128)(2,1)} %copy.52) | copy-start | bytes 786436
  468.4 2.3 copy-start
  468.4 3.5 copy-start.2
  475.2 207.5 %all-reduce.7.cloned.1.call-start = ((), (), s32[]{:S(2)}) async-start(), calls=%async_computation | async-start | bytes 1048576
  477.6 212.0 %copy-start.10 = (f32[2,16,1024]{2,1,0:T(8,128)S(1)}, f32[2,16,1024]{2,1,0:T(8,128)}, u32[]{:S(2)}) copy-start(f32[2,16,1024]{2,1,0:T(8,128)} %copy-done.9) | copy-start | bytes 393220
  480.1 211.1 %collective-permute-start.2 = (bf16[2,128,1024]{2,1,0:T(8,128)(2,1)}, bf16[2,128,1024]{2,1,0:T(8,128)(2,1)}, u32[]{:S(2)}, u32[]{:S(2)}) collective-permute-start(bf16[2,128,1024]{2,1,0:T(8,128)(2,1)} %get-tuple-element.381), channel_id=1, source_target_pairs={{0,1},{1,2},{2,3},{3,4},{4,5},{5,6},{6,7},{7,8},{8,9},{9,10},{10,1... | collective-permute-start | bytes 1572872 | tf_op jit(solution)/shard_map/ppermute | solution.py:40
  482.3 208.9 %collective-permute-start.3 = (bf16[2,128,1024]{2,1,0:T(8,128)(2,1)}, bf16[2,128,1024]{2,1,0:T(8,128)(2,1)}, u32[]{:S(2)}, u32[]{:S(2)}) collective-permute-start(bf16[2,128,1024]{2,1,0:T(8,128)(2,1)} %get-tuple-element.382), channel_id=1, source_target_pairs={{1,0},{2,1},{3,2},{4,3},{5,4},{6,5},{7,6},{8,7},{9,8},{10,9},{11,1... | collective-permute-start | bytes 1572872 | tf_op jit(solution)/shard_map/ppermute | solution.py:40
  693.6 8.1 %copy-start.7 = (f32[1,2,128,1024]{3,2,1,0:T(8,128)S(1)}, f32[1,2,128,1024]{3,2,1,0:T(8,128)}, u32[]{:S(2)}) copy-start(f32[1,2,128,1024]{3,2,1,0:T(8,128)} %fusion.46) | copy-start | bytes 3145732
  701.6 4.0 copy-start.3
  703.5 2.3 copy-start.1
  703.5 2.3 copy-start.13
Sparse Core Ops, SparseCore 0:
  475.3 132.1 all-reduce.8
  611.3 71.3 all-reduce.6
where the time goes:
time: 719 us; the launch traced here: 716 us
  matrix products  216 us (30%)
  waiting for transfers between devices  198 us (28%)
  local copies, waits for them, and re-layouts  132 us (18%)
  blocking collectives  117 us (16%)
  other arithmetic  26.1 us (4%)
  between operations  15.1 us (2%)
  starting transfers between devices  11.3 us (2%)
    unnamed x4, waiting for transfers between devices  198 us
    all_gather x1, blocking collectives, per_device(): top_all = lax.all_gather(top_local, ('grp', 'seq'), axis=1, tiled=True)  83.2 us
    dot_general x8, matrix products, one_pair(): jnp.einsum('hqk,qhd->khd', score_grad, query_part, preferred_element_type...  62 us
    dot_general x8, matrix products, one_pair(): jnp.einsum('hqk,khd->qhd', score_grad, key_part, preferred_element_type=j...  56 us
    all_gather x1, blocking collectives, per_device(): group_all = lax.all_gather(group_local, 'seq', axis=1, tiled=True)  33.8 us
    dynamic_slice x48, local copies, waits for them, and re-layouts, take_pair(): lax.dynamic_slice_in_dim(matrix, offset, pair_width, 1)  32.1 us
    sub x8, matrix products, one_pair(): unnormed = jnp.exp(scores - largest)  28 us
    dot_general x8, matrix products, one_pair(): jnp.einsum('hqk,khd->qhd', probs_low, value_part, preferred_element_type=...  25.9 us
  transfers between devices with their start and end apart: 6, of which 2 were waited for; matrix products, arithmetic and copies ran while one was open for 5% of the time, Pallas kernels for 0%

commit v1 on v0

v1 whole, which is shorter than its diff:
```python
import math

import jax
import jax.numpy as jnp
from jax import lax
from jax.experimental import pallas as pl
from jax.experimental.pallas import tpu as pltpu
from jax.sharding import PartitionSpec as P

H = 16
HD = 64
BLOCK = 512
P1 = 4
P2 = 32
RATIO = 8


EPS = 1e-06
NEG = -1e30


def extended(cells, sides, width):
    for axis, dim in sides:
        count = lax.axis_size(axis)
        ends = count - 1
        head = lax.slice_in_dim(cells, 0, width, axis=dim)
        tail = lax.slice_in_dim(cells, cells.shape[dim] - width, cells.shape[dim], axis=dim)
        cells = jnp.concatenate(
            [
                lax.ppermute(tail, axis, [(i, (i + 1) % count) for i in range(ends)]),
                cells,
                lax.ppermute(head, axis, [((i + 1) % count, i) for i in range(ends)]),
            ],
            axis=dim,
        )
    return cells


def shifted(block, axis, distance):
    devices = range(lax.axis_size(axis))
    route = [(i - distance, i) for i in devices if i - distance in devices]
    return lax.ppermute(block, axis, route)


def keep_bf16(value):
    rounded = lax.optimization_barrier(value.astype(jnp.bfloat16)).astype(jnp.float32)
    return value + lax.stop_gradient(rounded - value)


def pool_rows(stacked, factor):
    count_rows = stacked.shape[1] // factor
    return jnp.mean(
        stacked.reshape(2, count_rows, factor, stacked.shape[2]), axis=2, dtype=jnp.float32
    )


def normalize(pooled):
    shaped = pooled.reshape(pooled.shape[:-1] + (H, HD))
    scaled = shaped * lax.rsqrt(jnp.mean(shaped * shaped, axis=-1, keepdims=True) + EPS)
    return keep_bf16(scaled.reshape(pooled.shape))


def summary_back(pooled, upstream, factor):
    unused, pullback = jax.vjp(normalize, pooled)
    return jnp.repeat(pullback(upstream)[0] / factor, factor, axis=1)


PAIR = 2 * HD
CHUNK = 256


def dot(left, right):
    return jnp.dot(left, right, preferred_element_type=jnp.float32)


def attend_pair(lanes, live, query_ref, grad_ref, set_ref, score_ref, prob_ref, sgrad_ref):
    rows = query_ref.shape[0]
    count = set_ref.shape[1]
    spans = [(start, min(start + CHUNK, count)) for start in range(0, count, CHUNK)]
    query = query_ref[:, lanes].astype(jnp.float32) * (1.0 / math.sqrt(HD))
    query_t = query.T.astype(jnp.bfloat16)
    grad_t = grad_ref[:, lanes].astype(jnp.float32).T
    key_t = set_ref[0, :, lanes].T
    value_t = set_ref[1, :, lanes].T
    ones = jnp.ones((16, count), jnp.bfloat16)
    blank = jnp.zeros((HD, rows), jnp.bfloat16)
    outs, query_grads, scaled = [], [], []
    for head in range(2):
        part = slice(head * HD, (head + 1) * HD)

        def pad(half):
            return jnp.concatenate([half, blank] if head == 0 else [blank, half], axis=0)

        query_pad = pad(query_t[part])
        largest = None
        for start, stop in spans:
            scores = dot(set_ref[0, start:stop, lanes], query_pad)
            if start == BLOCK:
                scores = jnp.where(live, scores, NEG)
            score_ref[start:stop] = scores
            top = jnp.max(scores, axis=0, keepdims=True)
            largest = top if largest is None else jnp.maximum(largest, top)
        for start, stop in spans:
            prob_ref[head, start:stop] = jnp.exp(score_ref[start:stop] - largest).astype(
                jnp.bfloat16
            )
        mixed = dot(jnp.concatenate([value_t[part], ones], axis=0), prob_ref[head])
        inverse = 1.0 / mixed[HD : HD + 1]
        out = mixed[:HD] * inverse
        grad_scaled = (grad_t[part] * inverse).astype(jnp.bfloat16)
        delta = jnp.sum(grad_scaled.astype(jnp.float32) * out, axis=0, keepdims=True)
        grad_pad = pad(grad_scaled)
        for start, stop in spans:
            prob_grad = dot(set_ref[1, start:stop, lanes], grad_pad)
            sgrad_ref[head, start:stop] = prob_ref[head, start:stop] * (
                prob_grad - delta
            ).astype(jnp.bfloat16)
        outs.append(out)
        scaled.append(grad_scaled)
        query_grads.append(dot(key_t[part], sgrad_ref[head]) * (1.0 / math.sqrt(HD)))
    output = jnp.concatenate(outs, axis=0).T.astype(jnp.bfloat16)
    query_grad = jnp.concatenate(query_grads, axis=0).T.astype(jnp.bfloat16)
    grad_rows = jnp.concatenate(scaled, axis=0).astype(jnp.float32).T
    lower = lax.broadcasted_iota(jnp.int32, (rows, PAIR), 1) < HD

    def split(matrix):
        return (
            jnp.where(lower, matrix, 0.0).astype(jnp.bfloat16),
            jnp.where(lower, 0.0, matrix).astype(jnp.bfloat16),
        )

    grad_halves = split(grad_rows)
    query_halves = split(query)

    def row_grads(start, stop):
        key_grad = dot(sgrad_ref[0, start:stop], query_halves[0]) + dot(
            sgrad_ref[1, start:stop], query_halves[1]
        )
        value_grad = dot(prob_ref[0, start:stop], grad_halves[0]) + dot(
            prob_ref[1, start:stop], grad_halves[1]
        )
        return key_grad, value_grad

    return output, query_grad, row_grads, spans


def live_rows(number, total):
    row = lax.broadcasted_iota(jnp.int32, (CHUNK, 1), 0)
    before = row < CHUNK // 2
    dead = jnp.logical_or(
        jnp.logical_and(before, number == 0),
        jnp.logical_and(jnp.logical_not(before), number == total - 1),
    )
    return jnp.logical_not(dead)


def attend_kernel(
    query_ref, grad_ref, set_ref, out_ref, query_grad_ref, set_grad_ref,
    score_ref, prob_ref, sgrad_ref,
):
    seq_count = lax.axis_size("seq")
    number = lax.axis_index("grp") * seq_count + lax.axis_index("seq")
    live = live_rows(number, seq_count * lax.axis_size("grp"))

    def one_pair(pair, carry):
        lanes = pl.ds(pl.multiple_of(pair * PAIR, PAIR), PAIR)
        output, query_grad, row_grads, spans = attend_pair(
            lanes, live, query_ref, grad_ref, set_ref, score_ref, prob_ref, sgrad_ref
        )
        out_ref[:, lanes] = output
        query_grad_ref[:, lanes] = query_grad
        for start, stop in spans:
            key_grad, value_grad = row_grads(start, stop)
            set_grad_ref[0, start:stop, lanes] = key_grad
            set_grad_ref[1, start:stop, lanes] = value_grad
        return carry

    lax.fori_loop(0, query_ref.shape[1] // PAIR, one_pair, 0)


def attend_block(queries, out_grad, key_sets):
    rows, width = queries.shape
    count = key_sets.shape[1]
    whole = pl.BlockSpec(memory_space=pltpu.VMEM)
    return pl.pallas_call(
        attend_kernel,
        out_shape=(
            jax.ShapeDtypeStruct((rows, width), jnp.bfloat16),
            jax.ShapeDtypeStruct((rows, width), jnp.bfloat16),
            jax.ShapeDtypeStruct((2, count, width), jnp.float32),
        ),
        in_specs=[whole] * 3,
        out_specs=(whole,) * 3,
        scratch_shapes=[
            pltpu.VMEM((count, rows), jnp.float32),
            pltpu.VMEM((2, count, rows), jnp.bfloat16),
            pltpu.VMEM((2, count, rows), jnp.bfloat16),
        ],
        compiler_params=pltpu.CompilerParams(vmem_limit_bytes=56 * 2**20),
    )(queries, out_grad, key_sets)


def per_device(queries, keys, values, out_grad):
    frames = queries.shape[0]
    width_all = queries.shape[1]
    blocks = frames // BLOCK
    near_len = BLOCK // P1
    seq_count = lax.axis_size("seq")
    grp_count = lax.axis_size("grp")
    device = lax.axis_index("grp") * seq_count + lax.axis_index("seq")
    total_blocks = blocks * seq_count * grp_count
    stacked_kv = jnp.stack([keys, values])
    near_pooled = pool_rows(stacked_kv, P1)
    near_local = normalize(near_pooled).astype(jnp.bfloat16)
    near_ext = extended(near_local, ((("grp", "seq"), 1),), near_len)
    group_pooled = pool_rows(stacked_kv, P2)
    group_local = normalize(group_pooled).astype(jnp.bfloat16)
    group_all = lax.all_gather(group_local, "seq", axis=1, tiled=True)
    top_pooled = pool_rows(group_local, RATIO)
    top_local = normalize(top_pooled).astype(jnp.bfloat16)
    top_all = lax.all_gather(top_local, ("grp", "seq"), axis=1, tiled=True)
    group_len = group_all.shape[1]
    top_len = top_all.shape[1]
    key_count = BLOCK + 2 * near_len + group_len + top_len
    lower = BLOCK + 2 * near_len
    key_sets = jnp.concatenate(
        [stacked_kv, near_ext[:, :near_len], near_ext[:, 2 * near_len :], group_all, top_all],
        axis=1,
    )
    attended, query_grad, pair_grad = attend_block(queries, out_grad, key_sets)
    group_grad = pair_grad[:, lower : lower + group_len]
    top_grad = pair_grad[:, lower + group_len :]
    diag_total = pair_grad[:, :BLOCK]
    lower_rim = pair_grad[:, BLOCK : BLOCK + near_len]
    upper_rim = pair_grad[:, BLOCK + near_len : lower]
    from_next = shifted(lower_rim.astype(jnp.bfloat16), ("grp", "seq"), -1).astype(jnp.float32)
    from_prev = shifted(upper_rim.astype(jnp.bfloat16), ("grp", "seq"), 1).astype(jnp.float32)
    near_grad = from_next + from_prev
    top_own = lax.psum_scatter(top_grad, ("grp", "seq"), scatter_dimension=1, tiled=True)
    extra = summary_back(top_pooled, top_own, RATIO)
    group_own = (
        lax.psum_scatter(
            group_grad.astype(jnp.bfloat16), "seq", scatter_dimension=1, tiled=True
        ).astype(jnp.float32)
        + extra
    )
    kv_grad = (
        diag_total
        + summary_back(near_pooled, near_grad, P1)
        + summary_back(group_pooled, group_own, P2)
    )
    return (
        attended,
        query_grad,
        kv_grad[0].astype(jnp.bfloat16),
        kv_grad[1].astype(jnp.bfloat16),
    )


def solution(mesh):
    in_specs = (
        P(("grp", "seq"), None),
        P(("grp", "seq"), None),
        P(("grp", "seq"), None),
        P(("grp", "seq"), None),
    )
    out_specs = (
        P(("grp", "seq"), None),
        P(("grp", "seq"), None),
        P(("grp", "seq"), None),
        P(("grp", "seq"), None),
    )
    return jax.shard_map(
        per_device, mesh=mesh, in_specs=in_specs, out_specs=out_specs, check_vma=False
    )
```

time: 719 us -> 369 us (0.51)
  matrix products: 216 us -> 0 us
  local copies, waits for them, and re-layouts: 132 us -> 33.6 us
  waiting for transfers between devices: 198 us -> 126 us
  Pallas kernels: 0 us -> 38.2 us
    dot_general x40 -> x0, matrix products: 188 us -> none  [the longest x8 62 us: one_pair(): jnp.einsum('hqk,qhd->khd', score_grad, query_part, preferred_element_type...]
    unnamed x4 -> x3, waiting for transfers between devices: 198 us -> 126 us
    pallas_call x0 -> x1, Pallas kernels: none -> 38.2 us  [attend_block(): pl.pallas_call(attend_kernel, out_shape=(jax.ShapeDtypeStruct((rows, widt...]
    dynamic_update_slice x48 -> x0, local copies, waits for them, and re-layouts: 35.3 us -> none  [the longest x16 10.5 us: one_pair(): lax.dynamic_update_slice_in_dim(value_total, value_grad.reshape(rows_k, p...]
    dynamic_slice x48 -> x0, local copies, waits for them, and re-layouts: 32.1 us -> none  [take_pair(): lax.dynamic_slice_in_dim(matrix, offset, pair_width, 1)]
    sub x8 -> x0, matrix products: 28 us -> none  [one_pair(): unnormed = jnp.exp(scores - largest)]
    unnamed x40 -> x19, local copies, waits for them, and re-layouts: 13 us -> 5.63 us
  transfers between devices with their start and end apart: 6 -> 6, of which waited for: 2 -> 1; matrix products, arithmetic and copies ran while one was open for 5% -> 8% of each run, Pallas kernels for 0% -> 0%
where the time goes in v1:
time: 369 us; the launch traced here: 368 us
  waiting for transfers between devices  126 us (34%)
  blocking collectives  116 us (31%)
  Pallas kernels  38.2 us (10%)
  local copies, waits for them, and re-layouts  33.6 us (9%)
  other arithmetic  27.3 us (7%)
  between operations  15.8 us (4%)
  starting transfers between devices  10.4 us (3%)
    unnamed x3, waiting for transfers between devices  126 us
    all_gather x1, blocking collectives, per_device(): top_all = lax.all_gather(top_local, ('grp', 'seq'), axis=1, tiled=True)  84.8 us
    pallas_call x1, Pallas kernels, attend_block(): pl.pallas_call(attend_kernel, out_shape=(jax.ShapeDtypeStruct((rows, widt...  38.2 us
    all_gather x1, blocking collectives, per_device(): group_all = lax.all_gather(group_local, 'seq', axis=1, tiled=True)  31.3 us
    another operation x2, other arithmetic  10.5 us
  transfers between devices with their start and end apart: 6, of which 1 were waited for; matrix products, arithmetic and copies ran while one was open for 8% of the time, Pallas kernels for 0%

profile of v1, /device:TPU:0, one launch (start us, length us, event | category | flops | bytes accessed | tf_op | source)
XLA Modules:
  0.0 367.5 jit_solution(452250200341196813)
XLA Ops:
  8.0 0.0 all-reduce.3.cloned.1.call-start
  8.0 1.5 stack.24
  9.5 1.5 stack.25
  11.0 2.8 convert_reduce_fusion.1
  13.8 0.1 multiply_multiply_fusion.1
  13.9 0.3 copy.22
  14.3 0.1 bitcast_reduce_fusion.1
  14.4 1.0 mul.155
  15.4 1.6 copy.23
  17.1 0.2 fusion.4
  17.3 1.1 fusion.1
  18.4 1.3 collective-permute-start.1
  19.6 6.3 %collective-permute-start = (bf16[2,128,1024]{2,1,0:T(8,128)(2,1)}, bf16[2,128,1024]{2,1,0:T(8,128)(2,1)}, u32[]{:S(2)}, u32[]{:S(2)}) collective-permute-start(bf16[2,128,1024]{2,1,0:T(8,128)(2,1)} %fusion.1), channel_id=1, source_target_pairs={{0,1},{1,2},{2,3},{3,4},{4,5},{5,6},{6,7},{7,8},{8,9},{9,10},{10,1... | collective-permute-start | bytes 1572872 | tf_op jit(solution)/shard_map/ppermute | solution.py:30
  25.9 0.6 convert_reduce_fusion
  26.5 0.7 multiply_multiply_fusion.3
  27.2 1.0 mul.159
  28.2 0.7 reduce_sum.84
  28.9 0.7 fusion.12
  29.7 0.8 mul.160
  30.5 1.1 mul.161
  31.6 0.1 convert_reduce_fusion.2
  31.7 0.1 mul.164
  31.8 0.1 reduce_sum.86
  31.8 0.6 copy-done.6
  32.5 0.1 mul.165
  32.5 0.1 mul.166
  32.7 84.8 %all_gather.7 = bf16[2,64,1024]{2,0,1:T(2,128)(2,1)} all-gather(bf16[2,2,1024]{2,0,1:T(2,128)(2,1)S(1)} %copy.24), channel_id=1, replica_groups=mesh['grp'=4,'seq'=8] {'grp','seq'}, dimensions={1}, use_global_device_ids=true | all-gather | bytes 270336 | tf_op jit(solution)/shard_map/all_gather | solution.py:221
  117.5 1.4 maximum_dynamic-update-slice_fusion
  118.9 31.3 %all_gather.6 = bf16[2,128,1024]{2,1,0:T(8,128)(2,1)S(1)} all-gather(bf16[2,16,1024]{2,1,0:T(8,128)(2,1)S(1)} %get-tuple-element.11), channel_id=1, replica_groups=mesh['grp'=4,'seq'=8] {'seq'}, dimensions={1}, use_global_device_ids=true | all-gather | bytes 589824 | tf_op jit(solution)/shard_map/all_gather | solution.py:218
  150.2 1.1 constant_dynamic-update-slice_fusion.2
  151.3 1.1 constant_dynamic-update-slice_fusion.1
  152.4 0.1 copy_dynamic-update-slice_fusion.set_ref
  152.5 2.0 copy-done.2
  154.5 38.2 %shard_map.75 = (bf16[512,1024]{1,0:T(8,128)(2,1)}, bf16[512,1024]{1,0:T(8,128)(2,1)}, f32[2,960,1024]{2,1,0:T(8,128)}) custom-call(bf16[512,1024]{1,0:T(8,128)(2,1)} %query_ref.1, bf16[512,1024]{1,0:T(8,128)(2,1)} %grad_ref.1, bf16[2,960,1024]{2,1,0:T(8,128)(2,1)} %copy-done.2), custom_call_target="tpu_custom_call" | custom-call | tf_op jit(solution)/shard_map/pallas_call | solution.py:185
  192.6 1.9 slice.30
  194.5 5.8 %convert.10 = bf16[2,960,1024]{2,1,0:T(8,128)(2,1)} convert(f32[2,960,1024]{2,1,0:T(8,128)} %get-tuple-element.9) | non-fusion elementwise | flops 1966080 | bytes 11796480 | tf_op jit(solution)/shard_map/convert.5
  200.4 0.0 reduce-scatter.3.cloned.1.call-start
  200.4 2.5 fusion.18
  202.9 1.3 collective-permute-start.3
  204.3 1.5 collective-permute-start.2
  205.8 126.1 %all-reduce.3.cloned.1.call-done = f32[2,64,1024]{2,1,0:T(8,128)} async-done(((f32[2,64,1024]{2,1,0:T(8,128)}), f32[2,64,1024]{2,1,0:T(8,128)}) %all-reduce.3.cloned.1.call-update) | async-done | bytes 524304
  331.9 0.9 dynamic-slice_multiply_fusion
  332.8 0.1 mul.177
  332.8 0.1 reduce_sum.91
  333.0 0.1 broadcast_in_dim.33
  333.0 0.1 broadcast_in_dim.34
  333.1 0.9 fusion.10
  334.0 0.8 copy-done.3
  334.9 1.4 fusion.3
  336.3 1.3 copy.27
  337.6 1.3 bitcast_reduce_fusion
  338.9 1.0 broadcast_in_dim.30
  340.0 1.6 copy.28
  341.5 1.6 fusion.2
  343.2 3.2 broadcast_in_dim.32
  346.3 5.3 %reshape.119 = f32[2,512,1024]{2,1,0:T(8,128)} reshape(f32[2,128,4,1024]{3,2,1,0:T(4,128)} %broadcast_in_dim.32) | data formatting | bytes 8388608 | tf_op jit(solution)/shard_map/reshape | solution.py:65
  351.7 0.9 fusion.7
  352.5 0.1 mul.184
  352.6 0.1 reduce_sum.92
  352.8 0.1 broadcast_in_dim.36
  352.9 0.1 broadcast_in_dim.37
  353.1 0.9 fusion.6
  353.9 4.6 %fusion = bf16[2,512,1024]{2,1,0:T(8,128)(2,1)S(1)} fusion(f32[2,512,1024]{2,1,0:T(8,128)} %reshape.119, f32[2,960,1024]{2,1,0:T(8,128)} %get-tuple-element.9, f32[2,16,1024]{2,1,0:T(8,128)S(1)} %fusion.6), kind=kLoop, calls=%fused_computation.1 | loop fusion | flops 3145728 | bytes 10616832 | tf_op jit(solution)/shard_map/convert.2
  358.6 1.5 slice_bitcast_fusion
  (31 shorter events, 0.2 us)
Async XLA Ops:
  8.0 323.9 %all-reduce.3.cloned.1.call-start = ((), (), s32[]{:S(2)}) async-start(), calls=%async_computation.2 | async-start | bytes 1048576
  15.4 10.5 %copy-start = (bf16[512,1024]{1,0:T(8,128)(2,1)S(1)}, bf16[512,1024]{1,0:T(8,128)(2,1)}, u32[]{:S(2)}) copy-start(bf16[512,1024]{1,0:T(8,128)(2,1)} %param.6) | copy-start | bytes 3145732
  17.1 8.9 %copy-start.1 = (bf16[512,1024]{1,0:T(8,128)(2,1)S(1)}, bf16[512,1024]{1,0:T(8,128)(2,1)}, u32[]{:S(2)}) copy-start(bf16[512,1024]{1,0:T(8,128)(2,1)} %param.5) | copy-start | bytes 3145732
  18.4 132.9 %collective-permute-start.1 = (bf16[2,128,1024]{2,1,0:T(8,128)(2,1)}, bf16[2,128,1024]{2,1,0:T(8,128)(2,1)}, u32[]{:S(2)}, u32[]{:S(2)}) collective-permute-start(bf16[2,128,1024]{2,1,0:T(8,128)(2,1)} %fusion.1), channel_id=1, source_target_pairs={{1,0},{2,1},{3,2},{4,3},{5,4},{6,5},{7,6},{8,7},{9,8},{10,9},{11,1... | collective-permute-start | bytes 1572872 | tf_op jit(solution)/shard_map/ppermute | solution.py:32
  19.6 130.6 %collective-permute-start = (bf16[2,128,1024]{2,1,0:T(8,128)(2,1)}, bf16[2,128,1024]{2,1,0:T(8,128)(2,1)}, u32[]{:S(2)}, u32[]{:S(2)}) collective-permute-start(bf16[2,128,1024]{2,1,0:T(8,128)(2,1)} %fusion.1), channel_id=1, source_target_pairs={{0,1},{1,2},{2,3},{3,4},{4,5},{5,6},{6,7},{7,8},{8,9},{9,10},{10,1... | collective-permute-start | bytes 1572872 | tf_op jit(solution)/shard_map/ppermute | solution.py:30
  31.8 0.6 copy-start.6
  117.5 35.0 %copy-start.4 = (bf16[2,64,1024]{2,0,1:T(2,128)(2,1)S(1)}, bf16[2,64,1024]{2,0,1:T(2,128)(2,1)}, u32[]{:S(2)}) copy-start(bf16[2,64,1024]{2,0,1:T(2,128)(2,1)} %all_gather.7) | copy-start | bytes 786436
  152.5 2.0 copy-start.2
  200.3 132.6 %copy-start.7 = (f32[2,2,16]{2,1,0:T(2,128)S(1)}, f32[2,2,16]{2,1,0:T(2,128)}, u32[]{:S(2)}) copy-start(f32[2,2,16]{2,1,0:T(2,128)} %copy-done.6) | copy-start | bytes 772
  200.4 151.3 %reduce-scatter.3.cloned.1.call-start = ((), (), s32[]{:S(2)}) async-start(), calls=%async_computation.1 | async-start | bytes 589824 | tf_op jit(solution)/shard_map/reduce_scatter | solution.py:242
  202.9 131.1 %collective-permute-start.3 = (bf16[2,128,1024]{2,1,0:T(8,128)(2,1)}, bf16[2,128,1024]{2,1,0:T(8,128)(2,1)S(1)}, u32[]{:S(2)}, u32[]{:S(2)}) collective-permute-start(bf16[2,128,1024]{2,1,0:T(8,128)(2,1)} %get-tuple-element.13), channel_id=1, source_target_pairs={{0,1},{1,2},{2,3},{3,4},{4,5},{5,6},{6,7},{7,8},{8,9},{9,10},{10,1... | collective-permute-start | bytes 1572872 | tf_op jit(solution)/shard_map/ppermute | solution.py:42
  204.3 130.6 %collective-permute-start.2 = (bf16[2,128,1024]{2,1,0:T(8,128)(2,1)S(1)}, bf16[2,128,1024]{2,1,0:T(8,128)(2,1)}, u32[]{:S(2)}, u32[]{:S(2)}) collective-permute-start(bf16[2,128,1024]{2,1,0:T(8,128)(2,1)S(1)} %get-tuple-element.14), channel_id=1, source_target_pairs={{1,0},{2,1},{3,2},{4,3},{5,4},{6,5},{7,6},{8,7},{9,8},{10,9},{11,1... | collective-permute-start | bytes 1572872 | tf_op jit(solution)/shard_map/ppermute | solution.py:42
  334.0 0.8 copy-start.3
  346.3 6.4 %copy-start.5 = (f32[2,16,16]{2,1,0:T(8,128)S(1)}, f32[2,16,16]{2,1,0:T(8,128)}, u32[]{:S(2)}) copy-start(f32[2,16,16]{2,1,0:T(8,128)} %reduce_sum.84) | copy-start | bytes 6148
Sparse Core Ops, SparseCore 0:
  200.5 131.3 all-reduce.2
Sparse Core Ops, SparseCore 1:
  205.8 62.7 reduce-scatter.2

commit v2 on v1

v2 whole, which is shorter than its diff:
```python
import functools
import math

import jax
import jax.numpy as jnp
from jax import lax
from jax.experimental import pallas as pl
from jax.experimental.pallas import tpu as pltpu
from jax.sharding import PartitionSpec as P

HD = 64
BLOCK = 512
P1 = 4
P2 = 32
RATIO = 8
NEAR = BLOCK // P1
OWN = BLOCK // P2
SUMS = NEAR + OWN
GROUP_BASE = BLOCK + 2 * NEAR

EPS = 1e-06
NEG = -1e30
WIDTH = 256
MESH = pl.DeviceIdType.MESH
NEAR_F, GROUP_F, TOP_F, NEAR_B, GROUP_B, TOP_B = range(6)


PAIR = 2 * HD
CHUNK = 256


def dot(left, right):
    return jnp.dot(left, right, preferred_element_type=jnp.float32)


def attend_pair(lanes, live, query_ref, grad_ref, set_ref, score_ref, prob_ref, sgrad_ref):
    rows = query_ref.shape[0]
    count = set_ref.shape[1]
    spans = [(start, min(start + CHUNK, count)) for start in range(0, count, CHUNK)]
    query = query_ref[:, lanes].astype(jnp.float32) * (1.0 / math.sqrt(HD))
    query_t = query.T.astype(jnp.bfloat16)
    grad_t = grad_ref[:, lanes].astype(jnp.float32).T
    key_t = set_ref[0, :, lanes].T
    value_t = set_ref[1, :, lanes].T
    ones = jnp.ones((16, count), jnp.bfloat16)
    blank = jnp.zeros((HD, rows), jnp.bfloat16)
    outs, query_grads, scaled = [], [], []
    for head in range(2):
        part = slice(head * HD, (head + 1) * HD)

        def pad(half):
            return jnp.concatenate([half, blank] if head == 0 else [blank, half], axis=0)

        query_pad = pad(query_t[part])
        largest = None
        for start, stop in spans:
            scores = dot(set_ref[0, start:stop, lanes], query_pad)
            if start == BLOCK:
                scores = jnp.where(live, scores, NEG)
            score_ref[start:stop] = scores
            top = jnp.max(scores, axis=0, keepdims=True)
            largest = top if largest is None else jnp.maximum(largest, top)
        for start, stop in spans:
            prob_ref[head, start:stop] = jnp.exp(score_ref[start:stop] - largest).astype(
                jnp.bfloat16
            )
        mixed = dot(jnp.concatenate([value_t[part], ones], axis=0), prob_ref[head])
        inverse = 1.0 / mixed[HD : HD + 1]
        out = mixed[:HD] * inverse
        grad_scaled = (grad_t[part] * inverse).astype(jnp.bfloat16)
        delta = jnp.sum(grad_scaled.astype(jnp.float32) * out, axis=0, keepdims=True)
        grad_pad = pad(grad_scaled)
        for start, stop in spans:
            prob_grad = dot(set_ref[1, start:stop, lanes], grad_pad)
            sgrad_ref[head, start:stop] = prob_ref[head, start:stop] * (
                prob_grad - delta
            ).astype(jnp.bfloat16)
        outs.append(out)
        scaled.append(grad_scaled)
        query_grads.append(dot(key_t[part], sgrad_ref[head]) * (1.0 / math.sqrt(HD)))
    output = jnp.concatenate(outs, axis=0).T.astype(jnp.bfloat16)
    query_grad = jnp.concatenate(query_grads, axis=0).T.astype(jnp.bfloat16)
    grad_rows = jnp.concatenate(scaled, axis=0).astype(jnp.float32).T
    lower = lax.broadcasted_iota(jnp.int32, (rows, PAIR), 1) < HD

    def split(matrix):
        return (
            jnp.where(lower, matrix, 0.0).astype(jnp.bfloat16),
            jnp.where(lower, 0.0, matrix).astype(jnp.bfloat16),
        )

    grad_halves = split(grad_rows)
    query_halves = split(query)

    def row_grads(start, stop):
        key_grad = dot(sgrad_ref[0, start:stop], query_halves[0]) + dot(
            sgrad_ref[1, start:stop], query_halves[1]
        )
        value_grad = dot(prob_ref[0, start:stop], grad_halves[0]) + dot(
            prob_ref[1, start:stop], grad_halves[1]
        )
        return key_grad, value_grad

    return output, query_grad, row_grads, spans


def live_rows(number, total):
    row = lax.broadcasted_iota(jnp.int32, (CHUNK, 1), 0)
    before = row < CHUNK // 2
    dead = jnp.logical_or(
        jnp.logical_and(before, number == 0),
        jnp.logical_and(jnp.logical_not(before), number == total - 1),
    )
    return jnp.logical_not(dead)


def head_mean(matrix):
    width = matrix.shape[1]
    row = lax.broadcasted_iota(jnp.int32, (width, width), 0)
    column = lax.broadcasted_iota(jnp.int32, (width, width), 1)
    block = jnp.where((row >> 6) == (column >> 6), 1.0 / HD, 0.0).astype(jnp.float32)
    return jnp.dot(
        matrix, block, preferred_element_type=jnp.float32, precision=lax.Precision.HIGHEST
    )


def normalize(pooled):
    root = lax.rsqrt(head_mean(pooled * pooled) + EPS)
    return pooled * root, root


def pull_back(unit, root, upstream):
    return root * (upstream - unit * head_mean(unit * upstream))


def pool_matrix(transposed):
    shape = (BLOCK, SUMS) if transposed else (SUMS, BLOCK)
    summary = lax.broadcasted_iota(jnp.int32, shape, 1 if transposed else 0)
    frame = lax.broadcasted_iota(jnp.int32, shape, 0 if transposed else 1)
    near = jnp.where((frame >> 2) == summary, 1.0 / P1, 0.0)
    group = jnp.where((frame >> 5) == summary - NEAR, 1.0 / P2, 0.0)
    return jnp.where(summary < NEAR, near, group).astype(jnp.bfloat16)


def top_matrix(tops, transposed):
    shape = (tops * RATIO, tops) if transposed else (tops, tops * RATIO)
    summary = lax.broadcasted_iota(jnp.int32, shape, 1 if transposed else 0)
    member = lax.broadcasted_iota(jnp.int32, shape, 0 if transposed else 1)
    return jnp.where((member >> 3) == summary, 1.0 / RATIO, 0.0).astype(jnp.bfloat16)


def layer_kernel(
    grp_count, seq_count,
    query_ref, key_ref, value_ref, grad_ref,
    out_ref, query_grad_ref, key_grad_ref, value_grad_ref,
    set_ref, near_ref, unit_ref, root_ref, top_unit_ref, top_root_ref,
    score_ref, prob_ref, sgrad_ref, diag_ref, group_sum_ref,
    near_out, near_in, group_out, group_in, top_out, top_in,
    send_sem, recv_sem,
):
    grp, seq = lax.axis_index("grp"), lax.axis_index("seq")
    total = grp_count * seq_count
    number = grp * seq_count + seq
    after, before = lax.rem(number + 1, total), lax.rem(number + total - 1, total)
    after_id = (after // seq_count, lax.rem(after, seq_count))
    before_id = (before // seq_count, lax.rem(before, seq_count))
    seq_peers = [lax.rem(seq + step, seq_count) for step in range(1, seq_count)]
    grp_peers = [lax.rem(grp + step, grp_count) for step in range(1, grp_count)]
    tops = 2 * seq_count
    top_base = GROUP_BASE + OWN * seq_count
    parts = query_ref.shape[1] // WIDTH
    live = live_rows(number, total)
    sources = (key_ref, value_ref)

    everyone = [after_id, before_id]
    everyone += [(grp, peer) for peer in seq_peers] + [(peer, seq) for peer in grp_peers]
    barrier = pltpu.get_barrier_semaphore()
    for peer in everyone:
        pl.semaphore_signal(barrier, inc=1, device_id=peer, device_id_type=MESH)

    def cols_of(part):
        return pl.ds(pl.multiple_of(part * WIDTH, WIDTH), WIDTH)

    def rows_of(start, step, index):
        return pl.ds(pl.multiple_of(start + index * step, step), step)

    def send(kind, part, source, target, peer):
        pltpu.make_async_remote_copy(
            src_ref=source,
            dst_ref=target,
            send_sem=send_sem.at[kind, part],
            recv_sem=recv_sem.at[kind, part],
            device_id=peer,
            device_id_type=MESH,
        ).start()

    def wait(kind, part, sems):
        cols = cols_of(part)
        if kind == NEAR_F:
            view = set_ref.at[:, BLOCK:GROUP_BASE, cols]
        elif kind == GROUP_F:
            view = set_ref.at[:, GROUP_BASE : GROUP_BASE + OWN * (seq_count - 1), cols]
        elif kind == TOP_F:
            view = set_ref.at[:, top_base : top_base + tops * (grp_count - 1), cols]
        else:
            view = {NEAR_B: near_in, GROUP_B: group_in, TOP_B: top_in}[kind]
            view = view.at[:, :, :, cols]
        pltpu.make_async_copy(view, view, sems.at[kind, part]).wait()

    pool = pool_matrix(False)

    def summarize_part(part, carry):
        cols = cols_of(part)
        own = rows_of(GROUP_BASE, OWN, seq)
        for side in range(2):
            rows = sources[side][:, cols]
            set_ref[side, :BLOCK, cols] = rows
            unit, root = normalize(dot(pool, rows))
            unit_ref[side, :, cols] = unit
            root_ref[side, :, cols] = root
            near_ref[side, :, cols] = unit[:NEAR].astype(jnp.bfloat16)
            set_ref[side, own, cols] = unit[NEAR:].astype(jnp.bfloat16)

        @pl.when(part == 0)
        def _():
            pl.semaphore_wait(barrier, len(everyone))

        for peer in seq_peers:
            block = set_ref.at[:, own, cols]
            send(GROUP_F, part, block, block, (grp, peer))
        block = near_ref.at[:, :, cols]
        send(NEAR_F, part, block, set_ref.at[:, BLOCK : BLOCK + NEAR, cols], after_id)
        send(NEAR_F, part, block, set_ref.at[:, BLOCK + NEAR : GROUP_BASE, cols], before_id)
        return carry

    def top_part(part, carry):
        cols = cols_of(part)
        mine = rows_of(top_base, tops, grp)
        wait(GROUP_F, part, recv_sem)
        matrix = top_matrix(tops, False)
        for side in range(2):
            unit, root = normalize(dot(matrix, set_ref[side, GROUP_BASE:top_base, cols]))
            top_unit_ref[side, :, cols] = unit
            top_root_ref[side, :, cols] = root
            set_ref[side, mine, cols] = unit.astype(jnp.bfloat16)
        for peer in grp_peers:
            block = set_ref.at[:, mine, cols]
            send(TOP_F, part, block, block, (peer, seq))
        return carry

    def attend_part(part):
        cols = cols_of(part)
        wait(NEAR_F, part, recv_sem)
        wait(TOP_F, part, recv_sem)

        def one_pair(pair, carry):
            lanes = pl.ds(pl.multiple_of(part * WIDTH + pair * PAIR, PAIR), PAIR)
            output, query_grad, row_grads, spans = attend_pair(
                lanes, live, query_ref, grad_ref, set_ref, score_ref, prob_ref, sgrad_ref
            )
            out_ref[:, lanes] = output
            query_grad_ref[:, lanes] = query_grad
            for start, stop in spans:
                both = row_grads(start, stop)
                for side in range(2):
                    rows = both[side]
                    if stop <= BLOCK:
                        diag_ref[side, start:stop, lanes] = rows
                    elif stop <= GROUP_BASE:
                        near_out[0, side, :, lanes] = rows[:NEAR].astype(jnp.bfloat16)
                        near_out[1, side, :, lanes] = rows[NEAR:].astype(jnp.bfloat16)
                    else:
                        cut = max(0, min(stop, top_base) - start)
                        if cut:
                            low = start - GROUP_BASE
                            group_sum_ref[side, low : low + cut, lanes] = rows[:cut]
                        if start + cut < stop:
                            low, high = start + cut - top_base, stop - top_base
                            top_out[side, low:high, lanes] = rows[cut:].astype(jnp.bfloat16)
            return carry

        lax.fori_loop(0, WIDTH // PAIR, one_pair, 0)
        for slot, peer in enumerate(grp_peers):
            block = top_out.at[:, rows_of(0, tops, peer), cols]
            send(TOP_B, part, block, top_in.at[slot, :, :, cols], (peer, seq))
        send(NEAR_B, part, near_out.at[0, :, :, cols], near_in.at[0, :, :, cols], before_id)
        send(NEAR_B, part, near_out.at[1, :, :, cols], near_in.at[1, :, :, cols], after_id)

    def group_part(part):
        cols = cols_of(part)
        wait(TOP_B, part, recv_sem)
        spread = top_matrix(tops, True)
        for side in range(2):
            upstream = top_out[side, rows_of(0, tops, grp), cols].astype(jnp.float32)
            for slot in range(grp_count - 1):
                upstream += top_in[slot, side, :, cols].astype(jnp.float32)
            back = pull_back(top_unit_ref[side, :, cols], top_root_ref[side, :, cols], upstream)
            group_out[side, :, cols] = (
                group_sum_ref[side, :, cols] + dot(spread, back.astype(jnp.bfloat16))
            ).astype(jnp.bfloat16)
        for slot, peer in enumerate(seq_peers):
            block = group_out.at[:, rows_of(0, OWN, peer), cols]
            send(GROUP_B, part, block, group_in.at[slot, :, :, cols], (grp, peer))

    def final_part(part):
        cols = cols_of(part)
        wait(NEAR_B, part, recv_sem)
        wait(GROUP_B, part, recv_sem)
        spread = pool_matrix(True)
        for side, result in enumerate((key_grad_ref, value_grad_ref)):
            near = near_in[0, side, :, cols].astype(jnp.float32)
            near += near_in[1, side, :, cols].astype(jnp.float32)
            group = group_out[side, rows_of(0, OWN, seq), cols].astype(jnp.float32)
            for slot in range(seq_count - 1):
                group += group_in[slot, side, :, cols].astype(jnp.float32)
            upstream = jnp.concatenate([near, group], axis=0)
            back = pull_back(unit_ref[side, :, cols], root_ref[side, :, cols], upstream)
            result[:, cols] = (
                diag_ref[side, :, cols] + dot(spread, back.astype(jnp.bfloat16))
            ).astype(jnp.bfloat16)

    lax.fori_loop(0, parts, summarize_part, 0)
    lax.fori_loop(0, parts, top_part, 0)

    def stage(index, carry):
        @pl.when(index < parts)
        def _():
            attend_part(index)

        @pl.when(jnp.logical_and(index >= 1, index <= parts))
        def _():
            group_part(index - 1)

        @pl.when(index >= 2)
        def _():
            final_part(index - 2)

        return carry

    lax.fori_loop(0, parts + 2, stage, 0)
    for part in range(parts):
        for kind in range(6):
            wait(kind, part, send_sem)


def per_device(grp_count, seq_count, queries, keys, values, out_grad):
    rows, width = queries.shape
    group_rows = OWN * seq_count
    tops = 2 * seq_count
    count = GROUP_BASE + group_rows + tops * grp_count
    parts = width // WIDTH
    whole = pl.BlockSpec(memory_space=pltpu.VMEM)
    shape = jax.ShapeDtypeStruct((rows, width), jnp.bfloat16)
    low, high = jnp.bfloat16, jnp.float32
    return pl.pallas_call(
        functools.partial(layer_kernel, grp_count, seq_count),
        out_shape=(shape,) * 4,
        in_specs=[whole] * 4,
        out_specs=(whole,) * 4,
        scratch_shapes=[
            pltpu.VMEM((2, count, width), low),
            pltpu.VMEM((2, NEAR, width), low),
            pltpu.VMEM((2, SUMS, width), high),
            pltpu.VMEM((2, SUMS, width), high),
            pltpu.VMEM((2, tops, width), high),
            pltpu.VMEM((2, tops, width), high),
            pltpu.VMEM((count, rows), high),
            pltpu.VMEM((2, count, rows), low),
            pltpu.VMEM((2, count, rows), low),
            pltpu.VMEM((2, rows, width), high),
            pltpu.VMEM((2, group_rows, width), high),
            pltpu.VMEM((2, 2, NEAR, width), low),
            pltpu.VMEM((2, 2, NEAR, width), low),
            pltpu.VMEM((2, group_rows, width), low),
            pltpu.VMEM((seq_count - 1, 2, OWN, width), low),
            pltpu.VMEM((2, tops * grp_count, width), low),
            pltpu.VMEM((grp_count - 1, 2, tops, width), low),
            pltpu.SemaphoreType.DMA((6, parts)),
            pltpu.SemaphoreType.DMA((6, parts)),
        ],
        compiler_params=pltpu.CompilerParams(
            vmem_limit_bytes=60 * 2**20, collective_id=0, has_side_effects=True
        ),
    )(queries, keys, values, out_grad)


def solution(mesh):
    spec = P(("grp", "seq"), None)
    return jax.shard_map(
        functools.partial(per_device, mesh.shape["grp"], mesh.shape["seq"]),
        mesh=mesh,
        in_specs=(spec,) * 4,
        out_specs=(spec,) * 4,
        check_vma=False,
    )
```

time: 369 us -> 92.5 us (0.25)
  waiting for transfers between devices: 126 us -> 0 us
  blocking collectives: 116 us -> 0 us
  Pallas kernels: 38.2 us -> 85.1 us
  other arithmetic: 27.3 us -> 0 us
  local copies, waits for them, and re-layouts: 33.6 us -> 6.53 us
  between operations: 15.8 us -> 0.65 us
  starting transfers between devices: 10.4 us -> 0 us
    unnamed x3 -> x0, waiting for transfers between devices: 126 us -> none
    all_gather x2 -> x0, blocking collectives: 116 us -> none  [the longest x1 84.8 us: per_device(): top_all = lax.all_gather(top_local, ('grp', 'seq'), axis=1, tiled=True)]
    pallas_call x1, Pallas kernels: 38.2 us -> 85.1 us  [per_device(): pl.pallas_call(functools.partial(layer_kernel, grp_count, seq_count), out...]
    another operation x2 -> x0, other arithmetic: 10.5 us -> none
    ppermute x4 -> x0, starting transfers between devices: 10.4 us -> none  [the longest x1 6.29 us: extended(): lax.ppermute(tail, axis, [(i, (i + 1) % count) for i in range(ends)])]
    mul x12 -> x0, local copies, waits for them, and re-layouts: 7.65 us -> none  [the longest x9 6.23 us: normalize(): shaped * lax.rsqrt(jnp.mean(shaped * shaped, axis=-1, keepdims=True) + EPS)]
    broadcast_in_dim x7 -> x0, local copies, waits for them, and re-layouts: 6.18 us -> none  [the longest x1 3.18 us: summary_back(): return jnp.repeat(pullback(upstream)[0] / factor, factor, axis=1)]
    reduce_sum x9 -> x0, other arithmetic: 5.94 us -> none  [the longest x3 3.48 us: pool_rows(): jnp.mean(stacked.reshape(2, count_rows, factor, stacked.shape[2]), axis=2...]
  transfers between devices with their start and end apart: 6 -> 0, of which waited for: 1 -> 0; matrix products, arithmetic and copies ran while one was open for 8% -> 0% of each run, Pallas kernels for 0% -> 0%
where the time goes in v2:
time: 92.5 us; the launch traced here: 92.3 us
  Pallas kernels  85.1 us (92%)
  local copies, waits for them, and re-layouts  6.53 us (7%)
    pallas_call x1, Pallas kernels, per_device(): pl.pallas_call(functools.partial(layer_kernel, grp_count, seq_count), out...  85.1 us
    unnamed x10, local copies, waits for them, and re-layouts  6.53 us

profile of v2, /device:TPU:0, one launch (start us, length us, event | category | flops | bytes accessed | tf_op | source)
XLA Modules:
  0.0 92.3 jit_solution(16200850755533286353)
XLA Ops:
  0.6 85.1 %shard_map.75 = (bf16[512,1024]{1,0:T(8,128)(2,1)}, bf16[512,1024]{1,0:T(8,128)(2,1)}, bf16[512,1024]{1,0:T(8,128)(2,1)}, bf16[512,1024]{1,0:T(8,128)(2,1)}) custom-call(bf16[512,1024]{1,0:T(8,128)(2,1)} %query_ref.1, bf16[512,1024]{1,0:T(8,128)(2,1)} %key_ref.1, bf16[512,1024]{1,0:T(8,128)(2,1)} %value_ref.1, bf16[512,1024]{1,0:T(8,128)(2,1)} %grad_ref.1), custom_call_target="tpu_custom_call" | custom-call | tf_op jit(solution)/shard_map/pallas_call | solution.py:355
  85.7 0.0 copy-start.2
  85.8 2.4 %copy.12 = bf16[512,1024]{1,0:T(8,128)(2,1)} copy(bf16[512,1024]{1,0:T(8,128)(2,1)} %get-tuple-element.8) | data formatting | bytes 2097152
  88.1 0.0 copy-done.2
  88.1 0.0 copy-start.1
  88.1 1.0 %copy.13 = bf16[512,1024]{1,0:T(8,128)(2,1)} copy(bf16[512,1024]{1,0:T(8,128)(2,1)S(1)} %copy-done.2) | data formatting | bytes 2097152
  89.1 0.6 copy-done.1
  89.7 0.0 copy-start
  89.7 1.0 %copy.14 = bf16[512,1024]{1,0:T(8,128)(2,1)} copy(bf16[512,1024]{1,0:T(8,128)(2,1)S(1)} %copy-done.1) | data formatting | bytes 2097152
  90.7 0.6 copy-done
  91.3 1.0 %copy.15 = bf16[512,1024]{1,0:T(8,128)(2,1)} copy(bf16[512,1024]{1,0:T(8,128)(2,1)S(1)} %copy-done) | data formatting | bytes 2097152
Async XLA Ops:
  85.7 2.4 %copy-start.2 = (bf16[512,1024]{1,0:T(8,128)(2,1)S(1)}, bf16[512,1024]{1,0:T(8,128)(2,1)}, u32[]{:S(2)}) copy-start(bf16[512,1024]{1,0:T(8,128)(2,1)} %get-tuple-element.9) | copy-start | bytes 3145732
  88.1 1.6 %copy-start.1 = (bf16[512,1024]{1,0:T(8,128)(2,1)S(1)}, bf16[512,1024]{1,0:T(8,128)(2,1)}, u32[]{:S(2)}) copy-start(bf16[512,1024]{1,0:T(8,128)(2,1)} %get-tuple-element.10) | copy-start | bytes 3145732
  89.7 1.6 %copy-start = (bf16[512,1024]{1,0:T(8,128)(2,1)S(1)}, bf16[512,1024]{1,0:T(8,128)(2,1)}, u32[]{:S(2)}) copy-start(bf16[512,1024]{1,0:T(8,128)(2,1)} %get-tuple-element.11) | copy-start | bytes 3145732

commit v3 on v2

--- a/solution.py
+++ b/solution.py
@@ -118,10 +118,10 @@
     width = matrix.shape[1]
     row = lax.broadcasted_iota(jnp.int32, (width, width), 0)
     column = lax.broadcasted_iota(jnp.int32, (width, width), 1)
-    block = jnp.where((row >> 6) == (column >> 6), 1.0 / HD, 0.0).astype(jnp.float32)
-    return jnp.dot(
-        matrix, block, preferred_element_type=jnp.float32, precision=lax.Precision.HIGHEST
-    )
+    block = jnp.where((row >> 6) == (column >> 6), 1.0 / HD, 0.0).astype(jnp.bfloat16)
+    high = matrix.astype(jnp.bfloat16)
+    low = (matrix - high.astype(jnp.float32)).astype(jnp.bfloat16)
+    return dot(high, block) + dot(low, block)
 
 
 def normalize(pooled):
@@ -228,12 +228,19 @@
         for peer in seq_peers:
             block = set_ref.at[:, own, cols]
             send(GROUP_F, part, block, block, (grp, peer))
+        @pl.when(part > 0)
+        def _():
+            send_near(part - 1)
+
+        return carry
+
+    def send_near(part):
+        cols = cols_of(part)
         block = near_ref.at[:, :, cols]
         send(NEAR_F, part, block, set_ref.at[:, BLOCK : BLOCK + NEAR, cols], after_id)
         send(NEAR_F, part, block, set_ref.at[:, BLOCK + NEAR : GROUP_BASE, cols], before_id)
-        return carry
-
-    def top_part(part, carry):
+
+    def top_part(part):
         cols = cols_of(part)
         mine = rows_of(top_base, tops, grp)
         wait(GROUP_F, part, recv_sem)
@@ -246,7 +253,6 @@
         for peer in grp_peers:
             block = set_ref.at[:, mine, cols]
             send(TOP_F, part, block, block, (peer, seq))
-        return carry
 
     def attend_part(part):
         cols = cols_of(part)
@@ -254,6 +260,10 @@
         wait(TOP_F, part, recv_sem)
 
         def one_pair(pair, carry):
+            @pl.when(jnp.logical_and(pair == 1, part >= 1))
+            def _():
+                group_part(part - 1)
+
             lanes = pl.ds(pl.multiple_of(part * WIDTH + pair * PAIR, PAIR), PAIR)
             output, query_grad, row_grads, spans = attend_pair(
                 lanes, live, query_ref, grad_ref, set_ref, score_ref, prob_ref, sgrad_ref
@@ -277,14 +287,15 @@
                         if start + cut < stop:
                             low, high = start + cut - top_base, stop - top_base
                             top_out[side, low:high, lanes] = rows[cut:].astype(jnp.bfloat16)
+            for way, peer in enumerate((before_id, after_id)):
+                source = near_out.at[way, :, :, lanes]
+                send(NEAR_B, part, source, near_in.at[way, :, :, lanes], peer)
             return carry
 
         lax.fori_loop(0, WIDTH // PAIR, one_pair, 0)
         for slot, peer in enumerate(grp_peers):
             block = top_out.at[:, rows_of(0, tops, peer), cols]
             send(TOP_B, part, block, top_in.at[slot, :, :, cols], (peer, seq))
-        send(NEAR_B, part, near_out.at[0, :, :, cols], near_in.at[0, :, :, cols], before_id)
-        send(NEAR_B, part, near_out.at[1, :, :, cols], near_in.at[1, :, :, cols], after_id)
 
     def group_part(part):
         cols = cols_of(part)
@@ -320,14 +331,19 @@
             ).astype(jnp.bfloat16)
 
     lax.fori_loop(0, parts, summarize_part, 0)
-    lax.fori_loop(0, parts, top_part, 0)
+    send_near(parts - 1)
+    top_part(0)
 
     def stage(index, carry):
+        @pl.when(index + 1 < parts)
+        def _():
+            top_part(index + 1)
+
         @pl.when(index < parts)
         def _():
             attend_part(index)
 
-        @pl.when(jnp.logical_and(index >= 1, index <= parts))
+        @pl.when(index == parts)
         def _():
             group_part(index - 1)
 
@@ -341,6 +357,15 @@
     for part in range(parts):
         for kind in range(6):
             wait(kind, part, send_sem)
+
+
+def store_kernel(*refs):
+    sems = refs[8]
+    copies = [pltpu.make_async_copy(refs[i], refs[i + 4], sems.at[i]) for i in range(4)]
+    for copy in copies:
+        copy.start()
+    for copy in copies:
+        copy.wait()
 
 
 def per_device(grp_count, seq_count, queries, keys, values, out_grad):
@@ -352,7 +377,7 @@
     whole = pl.BlockSpec(memory_space=pltpu.VMEM)
     shape = jax.ShapeDtypeStruct((rows, width), jnp.bfloat16)
     low, high = jnp.bfloat16, jnp.float32
-    return pl.pallas_call(
+    results = pl.pallas_call(
         functools.partial(layer_kernel, grp_count, seq_count),
         out_shape=(shape,) * 4,
         in_specs=[whole] * 4,
@@ -382,6 +407,14 @@
             vmem_limit_bytes=60 * 2**20, collective_id=0, has_side_effects=True
         ),
     )(queries, keys, values, out_grad)
+    anywhere = pl.BlockSpec(memory_space=pltpu.HBM)
+    return pl.pallas_call(
+        store_kernel,
+        out_shape=(shape,) * 4,
+        in_specs=[anywhere] * 4,
+        out_specs=(anywhere,) * 4,
+        scratch_shapes=[pltpu.SemaphoreType.DMA((4,))],
+    )(*results)
 
 
 def solution(mesh):

time: 92.5 us -> 205 us (2.22)
  Pallas kernels: 85.1 us -> 204 us
  local copies, waits for them, and re-layouts: 6.53 us -> 0 us
    pallas_call x0 -> x1, Pallas kernels: none -> 128 us  [per_device(): pl.pallas_call(store_kernel, out_shape=(shape,) * 4, in_specs=[anywhere]...]
    pallas_call x1, Pallas kernels: 85.1 us -> 75.6 us  [per_device(): pl.pallas_call(functools.partial(layer_kernel, grp_count, seq_count), out...]
    unnamed x10 -> x0, local copies, waits for them, and re-layouts: 6.53 us -> none
where the time goes in v3:
time: 205 us; the launch traced here: 204 us
  Pallas kernels  204 us (100%)
    pallas_call x1, Pallas kernels, per_device(): pl.pallas_call(store_kernel, out_shape=(shape,) * 4, in_specs=[anywhere]...  128 us
    pallas_call x1, Pallas kernels, per_device(): pl.pallas_call(functools.partial(layer_kernel, grp_count, seq_count), out...  75.6 us

profile of v3, /device:TPU:0, one launch (start us, length us, event | category | flops | bytes accessed | tf_op | source)
XLA Modules:
  0.0 204.4 jit_solution(4159957538461738681)
XLA Ops:
  0.6 75.6 %shard_map.75 = (bf16[512,1024]{1,0:T(8,128)(2,1)}, bf16[512,1024]{1,0:T(8,128)(2,1)}, bf16[512,1024]{1,0:T(8,128)(2,1)}, bf16[512,1024]{1,0:T(8,128)(2,1)}) custom-call(bf16[512,1024]{1,0:T(8,128)(2,1)} %query_ref.1, bf16[512,1024]{1,0:T(8,128)(2,1)} %key_ref.1, bf16[512,1024]{1,0:T(8,128)(2,1)} %value_ref.1, bf16[512,1024]{1,0:T(8,128)(2,1)} %grad_ref.1), custom_call_target="tpu_custom_call" | custom-call | tf_op jit(solution)/shard_map/pallas_call | solution.py:380
  76.2 128.2 %shard_map.76 = (bf16[512,1024]{1,0:T(8,128)(2,1)}, bf16[512,1024]{1,0:T(8,128)(2,1)}, bf16[512,1024]{1,0:T(8,128)(2,1)}, bf16[512,1024]{1,0:T(8,128)(2,1)}) custom-call(bf16[512,1024]{1,0:T(8,128)(2,1)} %get-tuple-element.8.refs_0_, bf16[512,1024]{1,0:T(8,128)(2,1)} %get-tuple-element.9.refs_1_, bf16[512,1024]{1,0:T(8,128)(2,1)} %get-tuple-element.10.refs_2_, ...), custom_call_target="tpu_custom_call" | custom-call | tf_op jit(solution)/shard_map/pallas_call | solution.py:411

commit v4 on v3

--- a/solution.py
+++ b/solution.py
@@ -287,16 +287,18 @@
                         if start + cut < stop:
                             low, high = start + cut - top_base, stop - top_base
                             top_out[side, low:high, lanes] = rows[cut:].astype(jnp.bfloat16)
+            @pl.when(pair == WIDTH // PAIR - 1)
+            def _():
+                for slot, peer in enumerate(grp_peers):
+                    block = top_out.at[:, rows_of(0, tops, peer), cols]
+                    send(TOP_B, part, block, top_in.at[slot, :, :, cols], (peer, seq))
+
             for way, peer in enumerate((before_id, after_id)):
                 source = near_out.at[way, :, :, lanes]
                 send(NEAR_B, part, source, near_in.at[way, :, :, lanes], peer)
             return carry
 
         lax.fori_loop(0, WIDTH // PAIR, one_pair, 0)
-        for slot, peer in enumerate(grp_peers):
-            block = top_out.at[:, rows_of(0, tops, peer), cols]
-            send(TOP_B, part, block, top_in.at[slot, :, :, cols], (peer, seq))
-
     def group_part(part):
         cols = cols_of(part)
         wait(TOP_B, part, recv_sem)
@@ -360,12 +362,8 @@
 
 
 def store_kernel(*refs):
-    sems = refs[8]
-    copies = [pltpu.make_async_copy(refs[i], refs[i + 4], sems.at[i]) for i in range(4)]
-    for copy in copies:
-        copy.start()
-    for copy in copies:
-        copy.wait()
+    for i in range(4):
+        refs[i + 4][...] = refs[i][...]
 
 
 def per_device(grp_count, seq_count, queries, keys, values, out_grad):
@@ -407,13 +405,14 @@
             vmem_limit_bytes=60 * 2**20, collective_id=0, has_side_effects=True
         ),
     )(queries, keys, values, out_grad)
-    anywhere = pl.BlockSpec(memory_space=pltpu.HBM)
+    slab = pl.BlockSpec((rows // 4, width), lambda i: (i, 0))
     return pl.pallas_call(
         store_kernel,
         out_shape=(shape,) * 4,
-        in_specs=[anywhere] * 4,
-        out_specs=(anywhere,) * 4,
-        scratch_shapes=[pltpu.SemaphoreType.DMA((4,))],
+        grid=(4,),
+        in_specs=[slab] * 4,
+        out_specs=(slab,) * 4,
+        compiler_params=pltpu.CompilerParams(vmem_limit_bytes=60 * 2**20),
     )(*results)
 
 

time: 205 us -> 81.3 us (0.40)
  Pallas kernels: 204 us -> 80.5 us
    pallas_call x1, Pallas kernels: 128 us -> 4.66 us  [per_device(): pl.pallas_call(store_kernel, out_shape=(shape,) * 4, grid=(4,), in_specs=...]
where the time goes in v4:
time: 81.3 us; the launch traced here: 81.1 us
  Pallas kernels  80.5 us (99%)
    pallas_call x1, Pallas kernels, per_device(): pl.pallas_call(functools.partial(layer_kernel, grp_count, seq_count), out...  75.8 us
    pallas_call x1, Pallas kernels, per_device(): pl.pallas_call(store_kernel, out_shape=(shape,) * 4, grid=(4,), in_specs=...  4.66 us

profile of v4, /device:TPU:0, one launch (start us, length us, event | category | flops | bytes accessed | tf_op | source)
XLA Modules:
  0.0 81.1 jit_solution(3479190746224860068)
XLA Ops:
  0.6 75.8 %shard_map.75 = (bf16[512,1024]{1,0:T(8,128)(2,1)}, bf16[512,1024]{1,0:T(8,128)(2,1)}, bf16[512,1024]{1,0:T(8,128)(2,1)}, bf16[512,1024]{1,0:T(8,128)(2,1)}) custom-call(bf16[512,1024]{1,0:T(8,128)(2,1)} %query_ref.1, bf16[512,1024]{1,0:T(8,128)(2,1)} %key_ref.1, bf16[512,1024]{1,0:T(8,128)(2,1)} %value_ref.1, bf16[512,1024]{1,0:T(8,128)(2,1)} %grad_ref.1), custom_call_target="tpu_custom_call" | custom-call | tf_op jit(solution)/shard_map/pallas_call | solution.py:378
  76.4 4.7 %shard_map.76 = (bf16[512,1024]{1,0:T(8,128)(2,1)}, bf16[512,1024]{1,0:T(8,128)(2,1)}, bf16[512,1024]{1,0:T(8,128)(2,1)}, bf16[512,1024]{1,0:T(8,128)(2,1)}) custom-call(bf16[512,1024]{1,0:T(8,128)(2,1)} %get-tuple-element.8.refs_0_, bf16[512,1024]{1,0:T(8,128)(2,1)} %get-tuple-element.9.refs_1_, bf16[512,1024]{1,0:T(8,128)(2,1)} %get-tuple-element.10.refs_2_, ...), custom_call_target="tpu_custom_call" | custom-call | tf_op jit(solution)/shard_map/pallas_call | solution.py:409
